TPU v7x, 32 devices: a whole 2x2x4 slice. The times are simulated.
32 devices in a mesh: prow: 4 (over x, core), pcol: 8 (over z, y).
Axes of the slice: x: 2, y: 2, z: 4, core: 2. Of those that a mesh axis runs over, the one named last changes fastest.
Arguments:
- strip_quad: bfloat16 [4, 2048, 192, 128], P('prow', 'pcol'), may hold values from -0.4375 to 0.4375
- strip_weight: float32 [4, 2048, 192], P('prow', 'pcol'), may hold values from 0.25 to 4
- strip_dest: int32 [4, 2048, 1], P('prow', 'pcol'), may hold values from 0 to 7; in each aligned block of 256 rows (0 to 255, 256 to 511, ..., all dimensions but the last counted through in order) at most 48 rows name the same one
- strip_target: int32 [4, 2048], P('prow', 'pcol'), may hold values from 0 to 31
- strip_count: int32 [4, 8], P('prow', 'pcol'), may hold values from 1 to 256, 1536 in all within a row
- inner_quad: bfloat16 [4, 1024, 192, 128], P('prow', 'pcol'), may hold values from -0.4375 to 0.4375
- inner_weight: float32 [4, 1024, 192], P('prow', 'pcol'), may hold values from 0.25 to 4
- inner_target: int32 [4, 1024], P('prow', 'pcol'), may hold values from 0 to 31
- coarse_owner: int32 [4, 256], P('prow', 'pcol'), may hold values from 0 to 3
- panel_shift: float32 [4, 8, 128], P('prow', 'pcol'), may hold values from 2 to 64
Outputs:
- assembled: bfloat16 [4, 256, 128, 128], P('prow', 'pcol')
- coarse_block: float32 [4, 8, 128, 128], P('prow', 'pcol')
- panel_factor: float32 [4, 8, 128, 128], P('prow', 'pcol')
Inputs may be any that keep to these rules, and one draw needn't show every extreme that they name: `strip_dest`: in the 256 strip blocks of one subdomain no patch column is named more than 48 times; in some subdomain one is named exactly 48 times. `strip_count`: in each patch row the counts sum to 1536; strip blocks at or past the count are padding.
All inputs are finite; a program needn't handle non-finite values.
Results may differ from a plain program's by a relative error of at most 0.0035.
Values may be sent and summed in bfloat16 or wider, within the bound.
A program may use at most 320 MiB of HBM per device.

v0:
```python
import jax
import jax.numpy as jnp
from jax import lax
from jax.sharding import PartitionSpec as P


def tangents(quadrature, weight):
    scaled = (quadrature.astype(jnp.float32) * jnp.sqrt(weight)[..., None]).astype(jnp.bfloat16)
    return jnp.einsum("nqi,nqj->nij", scaled, scaled, preferred_element_type=jnp.float32).astype(
        jnp.bfloat16
    )


def place_blocks(strip_tangent, destination, valid_rows, target, columns, capacity):
    strip_rows = strip_tangent.shape[0]
    width = strip_tangent.shape[1]
    choose = (destination[:, None] == jnp.arange(columns, dtype=jnp.int32)[None, :]).astype(
        jnp.int32
    )
    before = jnp.cumsum(choose, axis=0) - choose
    slot_rank = jnp.sum(before * choose, axis=1)
    slot_place = destination * capacity + slot_rank
    placing = (
        jnp.arange(columns * capacity, dtype=jnp.int32)[:, None] == slot_place[None, :]
    ) & valid_rows[None, :]
    outgoing = jnp.dot(
        placing.astype(jnp.bfloat16),
        strip_tangent.reshape(strip_rows, width * width),
        preferred_element_type=jnp.float32,
    )
    outgoing = outgoing.astype(jnp.bfloat16).reshape(columns, capacity, width, width)
    labels = jnp.dot(
        placing.astype(jnp.float32), target.astype(jnp.float32), precision=lax.Precision.HIGHEST
    )
    labels = labels.astype(jnp.bfloat16).reshape(columns, capacity)
    return (outgoing, labels)


def sum_by_label(received, incoming_labels, slot_total):
    slot_index = jnp.arange(slot_total, dtype=jnp.float32)
    pick_strip = (
        slot_index[:, None] == incoming_labels.reshape(-1).astype(jnp.float32)[None, :]
    ).astype(jnp.bfloat16)
    return jnp.dot(pick_strip, received, preferred_element_type=jnp.float32)


def body(
    strip_quad,
    strip_weight,
    strip_dest,
    strip_target,
    strip_count,
    inner_quad,
    inner_weight,
    inner_target,
    coarse_owner,
    panel_shift,
):
    strip_rows = strip_quad.shape[1]
    inner_rows = inner_quad.shape[1]
    width = strip_quad.shape[3]
    slot_total = coarse_owner.shape[1]
    columns = lax.axis_size("pcol")
    row_total = lax.axis_size("prow")
    capacity = 3 * strip_rows // (2 * columns)
    strip_tangent = tangents(strip_quad[0], strip_weight[0])
    inner_tangent = tangents(inner_quad[0], inner_weight[0])
    destination = strip_dest[0, :, 0]
    position = jnp.arange(strip_rows, dtype=jnp.int32)
    valid_rows = position < strip_count[0, 0]
    outgoing, labels = place_blocks(
        strip_tangent, destination, valid_rows, strip_target[0], columns, capacity
    )
    received, incoming_labels = (
        lax.all_to_all(outgoing, "pcol", split_axis=0, concat_axis=0, tiled=True),
        lax.all_to_all(labels, "pcol", split_axis=0, concat_axis=0, tiled=True),
    )
    received = received.reshape(columns * capacity, width * width)
    strip_sum = sum_by_label(received, incoming_labels, slot_total)
    pick_inner = (
        jnp.arange(slot_total, dtype=jnp.int32)[:, None] == inner_target[0][None, :]
    ).astype(jnp.bfloat16)
    inner_sum = jnp.dot(
        pick_inner,
        inner_tangent.reshape(inner_rows, width * width),
        preferred_element_type=jnp.float32,
    )
    assembled = (strip_sum + inner_sum).astype(jnp.bfloat16)
    pick_owner = (
        jnp.arange(row_total, dtype=jnp.int32)[:, None] == coarse_owner[0][None, :]
    ).astype(jnp.bfloat16)
    partial_value = jnp.dot(pick_owner, assembled, preferred_element_type=jnp.float32)
    own_block = lax.psum_scatter(partial_value, "prow", scatter_dimension=0, tiled=True)
    coarse = own_block.reshape(width, width) / slot_total
    lead_block = assembled[0].reshape(width, width).astype(jnp.float32)
    panel_matrix = (
        lead_block + coarse + jnp.eye(width, dtype=jnp.float32) * panel_shift[0, 0][None, :]
    )
    factor = jnp.linalg.cholesky(panel_matrix)
    return (
        assembled.reshape(1, slot_total, width, width),
        coarse.reshape(1, 1, width, width),
        factor.reshape(1, 1, width, width),
    )


def solution(mesh):
    placed = (
        P("prow", "pcol", None, None),
        P("prow", "pcol", None),
        P("prow", "pcol", None),
        P("prow", "pcol"),
        P("prow", "pcol"),
        P("prow", "pcol", None, None),
        P("prow", "pcol", None),
        P("prow", "pcol"),
        P("prow", "pcol"),
        P("prow", "pcol", None),
    )
    return jax.shard_map(
        body,
        mesh=mesh,
        in_specs=placed,
        out_specs=(
            P("prow", "pcol", None, None),
            P("prow", "pcol", None, None),
            P("prow", "pcol", None, None),
        ),
        check_vma=False,
    )
```

profile of v0, /device:TPU:1, one launch (start us, length us, event | category | flops | bytes accessed | tf_op | source)
XLA Modules:
  0.0 422.6 jit_solution(17564475846274489876)
XLA Ops:
  7.2 0.7 fusion.40
  8.7 0.8 fusion.38
  9.4 0.7 multiply_add_fusion
  10.8 1.0 convolution_reduce_fusion
  11.8 0.7 all_to_all.12
  12.5 6.4 %all-to-all-start = ((bf16[8,1,48]{2,1,0:T(2,128)(2,1)}), bf16[8,1,48]{2,1,0:T(2,128)(2,1)S(1)}, u32[]{:S(2)}, u32[]{:S(2)}) async-start(bf16[8,1,48]{2,1,0:T(2,128)(2,1)} %all_to_all.12), calls=%async_computation | async-start | bytes 8192 | tf_op jit(solution)/shard_map/all_to_all | solution.py:76
  18.9 1.0 sqrt_bitcast_fusion
  20.0 11.5 %fusion.50 = bf16[256,192,128]{2,1,0:T(8,128)(2,1)} fusion(bf16[1,256,192,128]{3,2,1,0:T(8,128)(2,1)} %param.10, f32[256,192]{1,0:T(8,128)S(1)} %copy.27), kind=kLoop, calls=%fused_computation.1.clone.clone.clone.clone.2 | loop fusion | flops 18874368 | bytes 25362432 | tf_op jit(solution)/shard_map/nqi,nqj->nij/dot_general | solution.py:9
  31.5 16.4 %fusion.12 = bf16[256,128,128]{2,1,0:T(8,128)(2,1)} fusion(bf16[256,192,128]{2,1,0:T(8,128)(2,1)} %fusion.50), kind=kOutput, calls=%fused_computation.15 | convolution fusion | flops 1614807040 | bytes 20971520 | tf_op jit(solution)/shard_map/nqi,nqj->nij/dot_general | solution.py:9
  47.9 14.2 %fusion.19 = bf16[48,8,128,128]{3,1,2,0:T(8,128)(2,1)} fusion(bf16[32,8,128,128]{3,2,1,0:T(8,128)(2,1)} %bitcast.78, s32[256]{0:T(256)S(1)} %multiply_add_fusion, pred[256]{0:T(512)(128)(4,1)S(1)} %iota_compare_fusion.11), kind=kOutput, calls=%fused_computation.19 | convolution fusion | flops 3227713536 | bytes 20972800 | tf_op jit(solution)/shard_map/dot_general | solution.py:26
  62.0 11.5 %copy.35 = bf16[48,8,128,128]{3,2,1,0:T(8,128)(2,1)} copy(bf16[48,8,128,128]{3,1,2,0:T(8,128)(2,1)} %fusion.19) | data formatting | bytes 25165824
  73.6 5.6 %all-to-all-start.1 = ((bf16[8,48,128,128]{3,2,1,0:T(8,128)(2,1)}), bf16[8,48,128,128]{3,2,1,0:T(8,128)(2,1)}, u32[]{:S(2)}, u32[]{:S(2)}) async-start(bf16[8,48,128,128]{3,2,1,0:T(8,128)(2,1)} %bitcast.77), calls=%async_computation.1 | async-start | bytes 25165824 | tf_op jit(solution)/shard_map/all_to_all | solution.py:75
  79.5 15.3 %fusion.24 = bf16[128,128,128]{2,1,0:T(8,128)(2,1)} fusion(bf16[1,128,192,128]{3,2,1,0:T(8,128)(2,1)} %param.15, f32[128,192]{1,0:T(8,128)S(1)} %copy.28), kind=kOutput, calls=%fused_computation.22 | convolution fusion | flops 816840704 | bytes 10584064 | tf_op jit(solution)/shard_map/nqi,nqj->nij/dot_general | solution.py:9
  95.0 255.8 %all-to-all-done.1 = bf16[8,48,128,128]{3,2,1,0:T(8,128)(2,1)} async-done(((bf16[8,48,128,128]{3,2,1,0:T(8,128)(2,1)}), bf16[8,48,128,128]{3,2,1,0:T(8,128)(2,1)}, u32[]{:S(2)}, u32[]{:S(2)}) %all-to-all-start.1) | async-done | bytes 12582944 | tf_op jit(solution)/shard_map/all_to_all | solution.py:75
  350.8 13.4 %fusion.4 = f32[32,16384]{1,0:T(8,128)S(1)} fusion(bf16[48,8,128,128]{3,2,1,0:T(8,128)(2,1)} %bitcast.28, f32[384]{0:T(512)S(1)} %reshape.115), kind=kOutput, calls=%fused_computation.6 | convolution fusion | flops 402665472 | bytes 14681600 | tf_op jit(solution)/shard_map/dot_general | solution.py:44
  364.2 2.6 fusion.1
  366.8 1.0 fusion.41
  368.3 1.2 copy.38
  369.5 29.6 %all-reduce.3.cloned.1.call-done = f32[4,16384]{1,0:T(4,128)} async-done(((f32[4,16384]{1,0:T(4,128)}), f32[4,16384]{1,0:T(4,128)}) %all-reduce.3.cloned.1.call-update) | async-done | bytes 262160
  399.1 2.3 fusion.34
  401.8 11.7 %cholesky.19 = f32[128,128]{1,0:T(8,128)S(1)} custom-call(f32[128,128]{1,0:T(8,128)S(1)} %fusion.35), custom_call_target="Cholesky" | custom-call | tf_op jit(solution)/shard_map/jit(cholesky)/cholesky | solution.py:99
  413.8 0.6 compare_reduce_fusion
  414.4 0.7 select_bitcast_fusion
  415.1 0.7 copy.33
  (32 shorter events, 2.6 us)
Async XLA Ops:
  12.5 61.1 %all-to-all-start = ((bf16[8,1,48]{2,1,0:T(2,128)(2,1)}), bf16[8,1,48]{2,1,0:T(2,128)(2,1)S(1)}, u32[]{:S(2)}, u32[]{:S(2)}) async-start(bf16[8,1,48]{2,1,0:T(2,128)(2,1)} %all_to_all.12), calls=%async_computation | async-start | bytes 8192 | tf_op jit(solution)/shard_map/all_to_all | solution.py:76
  73.6 5.8 %copy-start.1 = (f32[1,128,192]{1,2,0:T(8,128)S(1)}, f32[1,128,192]{1,2,0:T(8,128)}, u32[]{:S(2)}) copy-start(f32[1,128,192]{1,2,0:T(8,128)} %param.16) | copy-start | bytes 294916
  73.6 277.2 %all-to-all-start.1 = ((bf16[8,48,128,128]{3,2,1,0:T(8,128)(2,1)}), bf16[8,48,128,128]{3,2,1,0:T(8,128)(2,1)}, u32[]{:S(2)}, u32[]{:S(2)}) async-start(bf16[8,48,128,128]{3,2,1,0:T(8,128)(2,1)} %bitcast.77), calls=%async_computation.1 | async-start | bytes 25165824 | tf_op jit(solution)/shard_map/all_to_all | solution.py:75
  79.1 320.0 %all-reduce.3.cloned.1.call-start = ((), (), s32[]{:S(2)}) async-start(), calls=%async_computation.2 | async-start | bytes 524288
  94.9 269.3 %copy-start.4 = (s32[1,128]{1,0:T(1,128)S(1)}, s32[1,128]{1,0:T(1,128)}, u32[]{:S(2)}) copy-start(s32[1,128]{1,0:T(1,128)} %param.17) | copy-start | bytes 1540
  350.8 13.4 %copy-start = (bf16[128,128,128]{2,1,0:T(8,128)(2,1)S(1)}, bf16[128,128,128]{2,1,0:T(8,128)(2,1)}, u32[]{:S(2)}) copy-start(bf16[128,128,128]{2,1,0:T(8,128)(2,1)} %fusion.24) | copy-start | bytes 12582916
  350.8 16.0 %copy-start.3 = (s32[1,32]{1,0:T(1,128)S(1)}, s32[1,32]{1,0:T(1,128)}, u32[]{:S(2)}) copy-start(s32[1,32]{1,0:T(1,128)} %param.18) | copy-start | bytes 388
  350.8 17.0 %copy-start.5 = (u32[32]{0:T(128)S(1)}, u32[32]{0:T(128)}, u32[]{:S(2)}) copy-start(u32[32]{0:T(128)} %constant.61) | copy-start | bytes 388
  350.8 50.8 %copy-start.2 = (f32[1,1,128]{2,1,0:T(1,128)S(1)}, f32[1,1,128]{2,1,0:T(1,128)}, u32[]{:S(2)}) copy-start(f32[1,1,128]{2,1,0:T(1,128)} %param.19) | copy-start | bytes 1540
Sparse Core Ops, SparseCore 0:
  367.9 31.2 all-reduce.2
where the time goes:
time: 425 us; the launch traced here: 423 us
  waiting for transfers between devices  285 us (67%)
  matrix products  63.8 us (15%)
  other arithmetic  29.9 us (7%)
  local copies, waits for them, and re-layouts  16.5 us (4%)
  between operations  14.8 us (3%)
  starting transfers between devices  12.2 us (3%)
    all_to_all x1, waiting for transfers between devices, body(): lax.all_to_all(outgoing, 'pcol', split_axis=0, concat_axis=0, tiled=True)  256 us
    dot_general x2, matrix products, tangents(): jnp.einsum('nqi,nqj->nij', scaled, scaled, preferred_element_type=jnp.flo...  31.7 us
    unnamed x2, waiting for transfers between devices  29.6 us
    dot_general x1, matrix products, place_blocks(): jnp.dot(placing.astype(jnp.bfloat16), strip_tangent.reshape(strip_rows, w...  14.2 us
    unnamed x16, local copies, waits for them, and re-layouts  14.1 us
    dot_general x1, matrix products, sum_by_label(): return jnp.dot(pick_strip, received, preferred_element_type=jnp.float32)  13.4 us
    another operation x3, other arithmetic, body(): factor = jnp.linalg.cholesky(panel_matrix)  12.5 us
    dot_general x1, other arithmetic, tangents(): jnp.einsum('nqi,nqj->nij', scaled, scaled, preferred_element_type=jnp.flo...  11.5 us
  transfers between devices with their start and end apart: 3, of which 2 were waited for; matrix products, arithmetic and copies ran while one was open for 17% of the time, Pallas kernels for 0%

commit v1 on v0

v1 whole, which is shorter than its diff:
```python
import functools
import jax
import jax.numpy as jnp
from jax import lax
from jax.experimental import pallas as pl
from jax.experimental.pallas import tpu as pltpu
from jax.sharding import PartitionSpec as P

MESH = pl.DeviceIdType.MESH
VMEM_LIMIT = 56 * 1024 * 1024
LANES = 128


def tangent_kernel(group, bucket_ref, weight_ref, quad_ref, out_ref, root, total, stage, sems):
    step = pl.program_id(0)
    buckets = total.shape[0] - 1
    chunk = stage.shape[1]

    @pl.when(step == 0)
    def _():
        root[...] = jnp.sqrt(weight_ref[...])

        @pl.loop(0, buckets + 1)
        def _(k):
            total[k] = jnp.zeros(total.shape[1:], total.dtype)

    @pl.loop(0, group // 8)
    def _(i):
        first = step * group + i * 8
        lane = lax.rem(first, LANES)
        tile = root[:, pl.ds(pl.multiple_of(first - lane, LANES), LANES)]
        tile = pltpu.roll(tile, lax.rem(LANES - lane, LANES), 1)
        for j in range(8):
            scaled = (quad_ref[i * 8 + j].astype(jnp.float32) * tile[:, j : j + 1]).astype(
                jnp.bfloat16
            )
            tangent = lax.dot_general(
                scaled, scaled, (((0,), (0,)), ((), ())), preferred_element_type=jnp.float32
            )
            bucket = bucket_ref[first + j]
            total[bucket] += tangent

    @pl.when(step == pl.num_programs(0) - 1)
    def _():
        copies = []
        for c in range(buckets // chunk):
            if c >= 2:
                copies[c - 2].wait()

            @pl.loop(0, chunk)
            def _(k):
                stage[c % 2, k] = total[c * chunk + k].astype(stage.dtype)

            copies.append(
                pltpu.make_async_copy(
                    stage.at[c % 2], out_ref.at[pl.ds(c * chunk, chunk)], sems.at[c % 2]
                )
            )
            copies[c].start()
        for copy in copies[-2:]:
            copy.wait()


def bucket_sums(quad, weight, bucket, buckets, chunk, dtype):
    count, rows, width = quad.shape
    group = 32
    return pl.pallas_call(
        functools.partial(tangent_kernel, group),
        out_shape=jax.ShapeDtypeStruct((buckets, width, width), dtype),
        grid_spec=pltpu.PrefetchScalarGridSpec(
            num_scalar_prefetch=1,
            grid=(count // group,),
            in_specs=[
                pl.BlockSpec((rows, count), lambda g, b: (0, 0)),
                pl.BlockSpec((group, rows, width), lambda g, b: (g, 0, 0)),
            ],
            out_specs=pl.BlockSpec(memory_space=pl.ANY),
            scratch_shapes=[
                pltpu.VMEM((rows, count), jnp.float32),
                pltpu.VMEM((buckets + 1, width, width), jnp.float32),
                pltpu.VMEM((2, chunk, width, width), dtype),
                pltpu.SemaphoreType.DMA((2,)),
            ],
        ),
        compiler_params=pltpu.CompilerParams(vmem_limit_bytes=VMEM_LIMIT),
    )(bucket, weight.T, quad)


def exchange_kernel(
    outer, inner_size, rows,
    out_ref, inner_ref, pick_ref, shift_ref,
    assembled_ref, coarse_ref, panel_ref,
    own, tot, near, line_out, line_in, part, part_in,
    load_sem, near_send, near_recv, line_send, line_recv, part_send, part_recv,
):
    slots = tot.shape[0]
    width = tot.shape[1]
    row, col = lax.axis_index("prow"), lax.axis_index("pcol")
    a, b = col // inner_size, col % inner_size
    f32 = jnp.float32

    barrier = pltpu.get_barrier_semaphore()

    def greet(r, c):
        pl.semaphore_signal(barrier, inc=1, device_id=(r, c), device_id_type=MESH)

    for j in range(1, inner_size):
        greet(row, a * inner_size + (b + j) % inner_size)
    for j in range(1, rows):
        greet((row + j) % rows, col)

    for j in (1, outer - 1):
        greet(row, (a + j) % outer * inner_size + b)

    pl.semaphore_wait(barrier, inner_size + rows)

    low = a < outer // 2

    def owner(s):
        if s == outer - 1:
            return a
        down = outer - 1 - s
        return jnp.where(
            low,
            jnp.where(down > a, down, down - 1),
            jnp.where(s < a, s, s + 1),
        )

    owners = [owner(s) for s in range(outer)]
    near_copies = []
    for s in range(outer):
        group = []
        for j in range(1, inner_size):
            peer = (b + j) % inner_size
            group.append(
                pltpu.make_async_remote_copy(
                    src_ref=out_ref.at[pl.ds((owners[s] * inner_size + peer) * slots, slots)],
                    dst_ref=near.at[inner_size - j - 1, s],
                    send_sem=near_send.at[inner_size - j - 1, s],
                    recv_sem=near_recv.at[inner_size - j - 1, s],
                    device_id=(row, a * inner_size + peer),
                    device_id_type=MESH,
                )
            )
        near_copies.append(group)
    for group in near_copies:
        for copy in group:
            copy.start()
    loads = [
        pltpu.make_async_copy(
            out_ref.at[pl.ds((owners[s] * inner_size + b) * slots, slots)],
            own.at[s],
            load_sem.at[s],
        )
        for s in range(outer)
    ]
    loads.append(pltpu.make_async_copy(inner_ref, tot, load_sem.at[outer]))
    for load in loads:
        load.start()

    def local(s, k):
        value = own[s, k].astype(f32)
        for j in range(inner_size - 1):
            value = value + near[j, s, k].astype(f32)
        return value

    line_copies = []
    for s in range(outer - 1):
        target = owners[s]
        up = target > a
        way = jnp.where(up, 0, 1)
        after = jnp.where(up, a + 1, a - 1)
        linked = jnp.where(up, a > 0, a < outer - 1)
        copy = pltpu.make_async_remote_copy(
            src_ref=line_out.at[s],
            dst_ref=line_in.at[way, target],
            send_sem=line_send.at[s],
            recv_sem=line_recv.at[way, target],
            device_id=(row, after * inner_size + b),
            device_id_type=MESH,
        )
        loads[s].wait()
        for near_copy in near_copies[s]:
            near_copy.wait_recv()

        @pl.when(linked)
        def _():
            copy.wait_recv()

            @pl.loop(0, slots)
            def _(k):
                value = local(s, k) + line_in[way, target, k].astype(f32)
                line_out[s, k] = value.astype(line_out.dtype)

        @pl.when(jnp.logical_not(linked))
        def _():
            @pl.loop(0, slots)
            def _(k):
                line_out[s, k] = local(s, k).astype(line_out.dtype)

        copy.start()
        line_copies.append(copy)

    last = outer - 1
    loads[last].wait()
    loads[outer].wait()
    for near_copy in near_copies[last]:
        near_copy.wait_recv()

    @pl.loop(0, slots)
    def _(k):
        tot[k] = tot[k] + local(last, k)

    for way, there in ((0, a > 0), (1, a < outer - 1)):

        @pl.when(there)
        def _():
            pltpu.make_async_remote_copy(
                src_ref=line_out.at[0],
                dst_ref=line_in.at[way, a],
                send_sem=line_send.at[0],
                recv_sem=line_recv.at[way, a],
                device_id=(row, a * inner_size + (b + 1) % inner_size),
                device_id_type=MESH,
            ).wait_recv()

            @pl.loop(0, slots)
            def _(k):
                tot[k] = tot[k] + line_in[way, a, k].astype(f32)

    part[...] = jnp.zeros_like(part)

    @pl.loop(0, slots)
    def _(k):
        block = tot[k].astype(jnp.bfloat16)
        assembled_ref[k] = block
        value = block.astype(f32)
        for r in range(rows):
            part[r] += pick_ref[r, k] * value

    part_copies = []
    for j in range(1, rows):
        peer = (row + j) % rows
        part_copies.append(
            pltpu.make_async_remote_copy(
                src_ref=part.at[peer],
                dst_ref=part_in.at[rows - j - 1],
                send_sem=part_send.at[rows - j - 1],
                recv_sem=part_recv.at[rows - j - 1],
                device_id=(peer, col),
                device_id_type=MESH,
            )
        )
    for copy in part_copies:
        copy.start()
    for copy in part_copies:
        copy.wait_recv()
    coarse = part[row]
    for j in range(rows - 1):
        coarse = coarse + part_in[j]
    coarse = coarse / slots
    coarse_ref[...] = coarse
    diagonal = lax.broadcasted_iota(jnp.int32, (width, width), 0) == lax.broadcasted_iota(
        jnp.int32, (width, width), 1
    )
    panel_ref[...] = (
        assembled_ref[0].astype(f32) + coarse + jnp.where(diagonal, shift_ref[...], 0.0)
    )
    for group in near_copies:
        for copy in group:
            copy.wait_send()
    for copy in line_copies + part_copies:
        copy.wait_send()


def exchange(outgoing, inner_sum, pick, shift, columns, rows):
    slots, width, _ = inner_sum.shape
    outer = 4
    inner_size = columns // outer
    f32, bf16 = jnp.float32, jnp.bfloat16
    block = (slots, width, width)
    dma = pltpu.SemaphoreType.DMA
    near = max(1, inner_size - 1)
    line = max(1, outer - 1)
    peers = max(1, rows - 1)
    vmem = pl.BlockSpec(memory_space=pltpu.VMEM)
    return pl.pallas_call(
        functools.partial(exchange_kernel, outer, inner_size, rows),
        out_shape=(
            jax.ShapeDtypeStruct(block, bf16),
            jax.ShapeDtypeStruct((width, width), f32),
            jax.ShapeDtypeStruct((width, width), f32),
        ),
        in_specs=[
            pl.BlockSpec(memory_space=pl.ANY),
            pl.BlockSpec(memory_space=pl.ANY),
            pl.BlockSpec(memory_space=pltpu.SMEM),
            vmem,
        ],
        out_specs=(vmem, vmem, vmem),
        scratch_shapes=[
            pltpu.VMEM((outer,) + block, bf16),
            pltpu.VMEM(block, f32),
            pltpu.VMEM((near, outer) + block, bf16),
            pltpu.VMEM((line,) + block, bf16),
            pltpu.VMEM((2, outer) + block, bf16),
            pltpu.VMEM((rows, width, width), f32),
            pltpu.VMEM((peers, width, width), f32),
            dma((outer + 1,)),
            dma((near, outer)),
            dma((near, outer)),
            dma((line,)),
            dma((2, outer)),
            dma((peers,)),
            dma((peers,)),
        ],
        compiler_params=pltpu.CompilerParams(
            collective_id=0, has_side_effects=True, vmem_limit_bytes=VMEM_LIMIT
        ),
    )(outgoing, inner_sum, pick, shift)


def body(
    strip_quad,
    strip_weight,
    strip_dest,
    strip_target,
    strip_count,
    inner_quad,
    inner_weight,
    inner_target,
    coarse_owner,
    panel_shift,
):
    strip_rows = strip_quad.shape[1]
    width = strip_quad.shape[3]
    slot_total = coarse_owner.shape[1]
    columns = lax.axis_size("pcol")
    row_total = lax.axis_size("prow")
    buckets = columns * slot_total
    position = jnp.arange(strip_rows, dtype=jnp.int32)
    bucket = jnp.where(
        position < strip_count[0, 0], strip_dest[0, :, 0] * slot_total + strip_target[0], buckets
    )
    outgoing = bucket_sums(
        strip_quad[0], strip_weight[0], bucket, buckets, slot_total, jnp.bfloat16
    )
    inner_sum = bucket_sums(
        inner_quad[0], inner_weight[0], inner_target[0], slot_total, slot_total // 2, jnp.float32
    )
    pick = (jnp.arange(row_total, dtype=jnp.int32)[:, None] == coarse_owner[0][None, :]).astype(
        jnp.float32
    )
    assembled, coarse, panel_matrix = exchange(
        outgoing, inner_sum, pick, panel_shift[0], columns, row_total
    )
    factor = jnp.linalg.cholesky(panel_matrix)
    return (
        assembled.reshape(1, slot_total, width, width),
        coarse.reshape(1, 1, width, width),
        factor.reshape(1, 1, width, width),
    )


def solution(mesh):
    placed = (
        P("prow", "pcol", None, None),
        P("prow", "pcol", None),
        P("prow", "pcol", None),
        P("prow", "pcol"),
        P("prow", "pcol"),
        P("prow", "pcol", None, None),
        P("prow", "pcol", None),
        P("prow", "pcol"),
        P("prow", "pcol"),
        P("prow", "pcol", None),
    )
    return jax.shard_map(
        body,
        mesh=mesh,
        in_specs=placed,
        out_specs=(
            P("prow", "pcol", None, None),
            P("prow", "pcol", None, None),
            P("prow", "pcol", None, None),
        ),
        check_vma=False,
    )
```

time: 425 us -> 185 us (0.44)
  waiting for transfers between devices: 285 us -> 0 us
  Pallas kernels: 0 us -> 161 us
  matrix products: 63.8 us -> 0 us
  between operations: 14.8 us -> 1.32 us
  other arithmetic: 29.9 us -> 17.7 us
  starting transfers between devices: 12.2 us -> 0 us
  local copies, waits for them, and re-layouts: 16.5 us -> 4.71 us
    all_to_all x2 -> x0, waiting for transfers between devices: 256 us -> none  [the longest x1 256 us: body(): lax.all_to_all(outgoing, 'pcol', split_axis=0, concat_axis=0, tiled=True)]
    pallas_call x0 -> x3, Pallas kernels: none -> 161 us  [the longest x1 107 us: exchange(): pl.pallas_call(functools.partial(exchange_kernel, outer, inner_size, rows...]
    dot_general x7 -> x0, matrix products: 63.8 us -> none  [the longest x2 31.7 us: tangents(): jnp.einsum('nqi,nqj->nij', scaled, scaled, preferred_element_type=jnp.flo...]
    unnamed x2 -> x0, waiting for transfers between devices: 29.6 us -> none
    all_to_all x2 -> x0, starting transfers between devices: 12 us -> none  [the longest x1 6.38 us: body(): lax.all_to_all(labels, 'pcol', split_axis=0, concat_axis=0, tiled=True)]
    dot_general x1 -> x0, other arithmetic: 11.5 us -> none  [tangents(): jnp.einsum('nqi,nqj->nij', scaled, scaled, preferred_element_type=jnp.flo...]
    unnamed x16 -> x2, local copies, waits for them, and re-layouts: 14.1 us -> 3.78 us
  transfers between devices with their start and end apart: 3 -> 0, of which waited for: 2 -> 0; matrix products, arithmetic and copies ran while one was open for 17% -> 0% of each run, Pallas kernels for 0% -> 0%
where the time goes in v1:
time: 185 us
  Pallas kernels  161 us (87%)
  other arithmetic  17.7 us (10%)
  local copies, waits for them, and re-layouts  4.71 us (3%)
    pallas_call x1, Pallas kernels, exchange(): pl.pallas_call(functools.partial(exchange_kernel, outer, inner_size, rows...  107 us
    pallas_call x2, Pallas kernels, bucket_sums(): pl.pallas_call(functools.partial(tangent_kernel, group), out_shape=jax.Sh...  54.3 us
    another operation x3, other arithmetic, body(): factor = jnp.linalg.cholesky(panel_matrix)  12.4 us
    unnamed x2, local copies, waits for them, and re-layouts  3.78 us

profile of v1, /device:TPU:1, one launch (start us, length us, event | category | flops | bytes accessed | tf_op | source)
XLA Modules:
  0.0 184.6 jit_solution(12096599469592327032)
XLA Ops:
  1.3 0.7 broadcast_multiply_fusion
  2.0 1.2 compare_select_fusion.bucket_ref
  3.2 1.2 fusion.1.pick_ref
  4.4 17.7 %shard_map.122.inner_ref = f32[32,128,128]{2,1,0:T(8,128)} custom-call(s32[128]{0:T(128)} %bitcast.31, f32[192,128]{1,0:T(8,128)} %bitcast.27, bf16[128,192,128]{2,1,0:T(8,128)(2,1)} %bitcast.24), custom_call_target="tpu_custom_call" | custom-call | tf_op jit(solution)/shard_map/pallas_call | solution.py:67
  22.2 36.6 %shard_map.121.out_ref = bf16[256,128,128]{2,1,0:T(8,128)(2,1)} custom-call(s32[256]{0:T(256)} %compare_select_fusion.bucket_ref, f32[192,256]{1,0:T(8,128)} %bitcast.26, bf16[256,192,128]{2,1,0:T(8,128)(2,1)} %bitcast.23), custom_call_target="tpu_custom_call" | custom-call | tf_op jit(solution)/shard_map/pallas_call | solution.py:67
  58.8 106.5 %shard_map.123 = (bf16[32,128,128]{2,1,0:T(8,128)(2,1)}, f32[128,128]{1,0:T(8,128)}, f32[128,128]{1,0:T(8,128)}) custom-call(bf16[256,128,128]{2,1,0:T(8,128)(2,1)} %shard_map.121.out_ref, f32[32,128,128]{2,1,0:T(8,128)} %shard_map.122.inner_ref, f32[4,32]{1,0:T(4,128)} %fusion.1.pick_ref, f32[1,128]{1,0:T(1,128)} %bitcast.32), custom_call_target="tpu_custom_call" | custom-call | tf_op jit(solution)/shard_map/pallas_call | solution.py:287
  165.3 0.9 copy.13
  166.2 0.9 fusion
  167.1 11.7 %cholesky.18 = f32[128,128]{1,0:T(8,128)S(1)} custom-call(f32[128,128]{1,0:T(8,128)S(1)} %fusion), custom_call_target="Cholesky" | custom-call | tf_op jit(solution)/shard_map/jit(cholesky)/cholesky | solution.py:357
  178.8 0.6 compare_reduce_fusion
  179.5 1.3 select_bitcast_fusion
  180.8 2.3 %copy.17 = bf16[1,32,128,128]{3,2,1,0:T(8,128)(2,1)} copy(bf16[1,32,128,128]{3,2,1,0:T(8,128)(2,1)} %bitcast.25) | data formatting | bytes 2097152
  183.1 1.5 copy.18
  (1 shorter events, 0.0 us)

commit v2 on v1

--- a/solution.py
+++ b/solution.py
@@ -7,94 +7,51 @@
 from jax.sharding import PartitionSpec as P
 
 MESH = pl.DeviceIdType.MESH
-VMEM_LIMIT = 56 * 1024 * 1024
-LANES = 128
-
-
-def tangent_kernel(group, bucket_ref, weight_ref, quad_ref, out_ref, root, total, stage, sems):
-    step = pl.program_id(0)
-    buckets = total.shape[0] - 1
-    chunk = stage.shape[1]
-
-    @pl.when(step == 0)
-    def _():
-        root[...] = jnp.sqrt(weight_ref[...])
-
-        @pl.loop(0, buckets + 1)
-        def _(k):
-            total[k] = jnp.zeros(total.shape[1:], total.dtype)
-
-    @pl.loop(0, group // 8)
-    def _(i):
-        first = step * group + i * 8
-        lane = lax.rem(first, LANES)
-        tile = root[:, pl.ds(pl.multiple_of(first - lane, LANES), LANES)]
-        tile = pltpu.roll(tile, lax.rem(LANES - lane, LANES), 1)
-        for j in range(8):
-            scaled = (quad_ref[i * 8 + j].astype(jnp.float32) * tile[:, j : j + 1]).astype(
-                jnp.bfloat16
-            )
-            tangent = lax.dot_general(
-                scaled, scaled, (((0,), (0,)), ((), ())), preferred_element_type=jnp.float32
-            )
-            bucket = bucket_ref[first + j]
-            total[bucket] += tangent
-
-    @pl.when(step == pl.num_programs(0) - 1)
-    def _():
-        copies = []
-        for c in range(buckets // chunk):
-            if c >= 2:
-                copies[c - 2].wait()
-
-            @pl.loop(0, chunk)
-            def _(k):
-                stage[c % 2, k] = total[c * chunk + k].astype(stage.dtype)
-
-            copies.append(
-                pltpu.make_async_copy(
-                    stage.at[c % 2], out_ref.at[pl.ds(c * chunk, chunk)], sems.at[c % 2]
-                )
-            )
-            copies[c].start()
-        for copy in copies[-2:]:
-            copy.wait()
-
-
-def bucket_sums(quad, weight, bucket, buckets, chunk, dtype):
-    count, rows, width = quad.shape
-    group = 32
-    return pl.pallas_call(
-        functools.partial(tangent_kernel, group),
-        out_shape=jax.ShapeDtypeStruct((buckets, width, width), dtype),
-        grid_spec=pltpu.PrefetchScalarGridSpec(
-            num_scalar_prefetch=1,
-            grid=(count // group,),
-            in_specs=[
-                pl.BlockSpec((rows, count), lambda g, b: (0, 0)),
-                pl.BlockSpec((group, rows, width), lambda g, b: (g, 0, 0)),
-            ],
-            out_specs=pl.BlockSpec(memory_space=pl.ANY),
-            scratch_shapes=[
-                pltpu.VMEM((rows, count), jnp.float32),
-                pltpu.VMEM((buckets + 1, width, width), jnp.float32),
-                pltpu.VMEM((2, chunk, width, width), dtype),
-                pltpu.SemaphoreType.DMA((2,)),
-            ],
+VMEM_LIMIT = 60 * 1024 * 1024
+UNROLL = 8
+
+
+def grouped(member, target, valid, groups, capacity, slots):
+    count = member.shape[0]
+    place = jnp.arange(count, dtype=jnp.int32)
+    key = target * count + place
+    peer = (member[:, None] == member[None, :]) & valid[None, :]
+    rank = jnp.sum((peer & (key[None, :] < key[:, None])).astype(jnp.int32), axis=1)
+    spot = jnp.where(valid, member * capacity + rank, groups * capacity)
+    at = spot[None, :] == jnp.arange(groups * capacity, dtype=jnp.int32)[:, None]
+    packed = jnp.sum(jnp.where(at, key[None, :], 0), axis=1).reshape(groups, capacity)
+    order, label = packed % count, packed // count
+    same = jnp.concatenate(
+        [jnp.zeros((groups, 1), jnp.bool_), label[:, 1:] == label[:, :-1]], axis=1
+    ).astype(jnp.float32)
+    bucket = jnp.where(valid, member * slots + target, groups * slots)
+    index = jnp.arange(groups * slots, dtype=jnp.int32)[:, None]
+    held = jnp.sum((bucket[None, :] == index).astype(jnp.int32), axis=1)
+    upto = jnp.sum(
+        ((bucket[None, :] <= index) & (bucket[None, :] >= index // slots * slots)).astype(
+            jnp.int32
         ),
-        compiler_params=pltpu.CompilerParams(vmem_limit_bytes=VMEM_LIMIT),
-    )(bucket, weight.T, quad)
+        axis=1,
+    )
+    last = jnp.maximum(upto - 1, 0).reshape(groups, slots)
+    some = (held > 0).astype(jnp.float32).reshape(groups, slots)
+    return order, same, last, some
 
 
 def exchange_kernel(
     outer, inner_size, rows,
-    out_ref, inner_ref, pick_ref, shift_ref,
+    strip_ref, inner_ref, strip_root, inner_root,
+    strip_order, strip_same, strip_last, strip_some,
+    inner_order, inner_same, inner_last, inner_some,
+    pick_ref, shift_ref,
     assembled_ref, coarse_ref, panel_ref,
-    own, tot, near, line_out, line_in, part, part_in,
+    quad, run, out, tot, near, line_out, line_in, part, part_in,
     load_sem, near_send, near_recv, line_send, line_recv, part_send, part_recv,
 ):
     slots = tot.shape[0]
     width = tot.shape[1]
+    load = pltpu.make_async_copy(strip_ref, quad, load_sem.at[0])
+    load.start()
     row, col = lax.axis_index("prow"), lax.axis_index("pcol")
     a, b = col // inner_size, col % inner_size
     f32 = jnp.float32
@@ -127,39 +84,51 @@
         )
 
     owners = [owner(s) for s in range(outer)]
+
+    def sum_runs(root, order, same, g):
+        def step(i, total):
+            for j in range(UNROLL):
+                p = i * UNROLL + j
+                n = order[g, p]
+                scaled = (quad[n].T.astype(f32) * root[n]).astype(jnp.bfloat16)
+                tangent = lax.dot_general(
+                    scaled, scaled, (((1,), (1,)), ((), ())), preferred_element_type=f32
+                )
+                total = total * same[g, p] + tangent
+                run[p] = total
+            return total
+
+        lax.fori_loop(0, order.shape[1] // UNROLL, step, jnp.zeros((width, width), f32))
+
+    load.wait()
     near_copies = []
     for s in range(outer):
         group = []
         for j in range(1, inner_size):
             peer = (b + j) % inner_size
-            group.append(
-                pltpu.make_async_remote_copy(
-                    src_ref=out_ref.at[pl.ds((owners[s] * inner_size + peer) * slots, slots)],
-                    dst_ref=near.at[inner_size - j - 1, s],
-                    send_sem=near_send.at[inner_size - j - 1, s],
-                    recv_sem=near_recv.at[inner_size - j - 1, s],
-                    device_id=(row, a * inner_size + peer),
-                    device_id_type=MESH,
-                )
+            target = owners[s] * inner_size + peer
+            sum_runs(strip_root, strip_order, strip_same, target)
+
+            @pl.loop(0, slots)
+            def _(k):
+                value = run[strip_last[target, k]] * strip_some[target, k]
+                out[j - 1, s, k] = value.astype(out.dtype)
+
+            copy = pltpu.make_async_remote_copy(
+                src_ref=out.at[j - 1, s],
+                dst_ref=near.at[inner_size - j - 1, s],
+                send_sem=near_send.at[inner_size - j - 1, s],
+                recv_sem=near_recv.at[inner_size - j - 1, s],
+                device_id=(row, a * inner_size + peer),
+                device_id_type=MESH,
             )
+            copy.start()
+            group.append(copy)
         near_copies.append(group)
-    for group in near_copies:
-        for copy in group:
-            copy.start()
-    loads = [
-        pltpu.make_async_copy(
-            out_ref.at[pl.ds((owners[s] * inner_size + b) * slots, slots)],
-            own.at[s],
-            load_sem.at[s],
-        )
-        for s in range(outer)
-    ]
-    loads.append(pltpu.make_async_copy(inner_ref, tot, load_sem.at[outer]))
-    for load in loads:
-        load.start()
 
     def local(s, k):
-        value = own[s, k].astype(f32)
+        mine = owners[s] * inner_size + b
+        value = run[strip_last[mine, k]] * strip_some[mine, k]
         for j in range(inner_size - 1):
             value = value + near[j, s, k].astype(f32)
         return value
@@ -179,7 +148,7 @@
             device_id=(row, after * inner_size + b),
             device_id_type=MESH,
         )
-        loads[s].wait()
+        sum_runs(strip_root, strip_order, strip_same, target * inner_size + b)
         for near_copy in near_copies[s]:
             near_copy.wait_recv()
 
@@ -202,14 +171,31 @@
         line_copies.append(copy)
 
     last = outer - 1
-    loads[last].wait()
-    loads[outer].wait()
+    sum_runs(strip_root, strip_order, strip_same, col)
+
+    @pl.loop(0, slots)
+    def _(k):
+        tot[k] = run[strip_last[col, k]] * strip_some[col, k]
+
+    load = pltpu.make_async_copy(inner_ref, quad.at[pl.ds(0, inner_ref.shape[0])], load_sem.at[1])
+    load.start()
+    load.wait()
+
+    @pl.loop(0, inner_order.shape[0])
+    def _(g):
+        sum_runs(inner_root, inner_order, inner_same, g)
+
+        @pl.loop(0, slots)
+        def _(k):
+            tot[k] += run[inner_last[g, k]] * inner_some[g, k]
+
     for near_copy in near_copies[last]:
         near_copy.wait_recv()
 
     @pl.loop(0, slots)
     def _(k):
-        tot[k] = tot[k] + local(last, k)
+        for j in range(inner_size - 1):
+            tot[k] += near[j, last, k].astype(f32)
 
     for way, there in ((0, a > 0), (1, a < outer - 1)):
 
@@ -273,8 +259,10 @@
         copy.wait_send()
 
 
-def exchange(outgoing, inner_sum, pick, shift, columns, rows):
-    slots, width, _ = inner_sum.shape
+def exchange(quads, roots, strip_plan, inner_plan, pick, shift, columns, rows):
+    slots = pick.shape[1]
+    width = shift.shape[1]
+    longest = max(strip_plan[0].shape[1], inner_plan[0].shape[1])
     outer = 4
     inner_size = columns // outer
     f32, bf16 = jnp.float32, jnp.bfloat16
@@ -294,19 +282,23 @@
         in_specs=[
             pl.BlockSpec(memory_space=pl.ANY),
             pl.BlockSpec(memory_space=pl.ANY),
-            pl.BlockSpec(memory_space=pltpu.SMEM),
             vmem,
-        ],
+            vmem,
+        ]
+        + [pl.BlockSpec(memory_space=pltpu.SMEM)] * 9
+        + [vmem],
         out_specs=(vmem, vmem, vmem),
         scratch_shapes=[
-            pltpu.VMEM((outer,) + block, bf16),
+            pltpu.VMEM(quads[0].shape, bf16),
+            pltpu.VMEM((longest, width, width), f32),
+            pltpu.VMEM((near, outer) + block, bf16),
             pltpu.VMEM(block, f32),
             pltpu.VMEM((near, outer) + block, bf16),
             pltpu.VMEM((line,) + block, bf16),
             pltpu.VMEM((2, outer) + block, bf16),
             pltpu.VMEM((rows, width, width), f32),
             pltpu.VMEM((peers, width, width), f32),
-            dma((outer + 1,)),
+            dma((2,)),
             dma((near, outer)),
             dma((near, outer)),
             dma((line,)),
@@ -317,7 +309,7 @@
         compiler_params=pltpu.CompilerParams(
             collective_id=0, has_side_effects=True, vmem_limit_bytes=VMEM_LIMIT
         ),
-    )(outgoing, inner_sum, pick, shift)
+    )(*quads, *roots, *strip_plan, *inner_plan, pick, shift)
 
 
 def body(
@@ -337,22 +329,29 @@
     slot_total = coarse_owner.shape[1]
     columns = lax.axis_size("pcol")
     row_total = lax.axis_size("prow")
-    buckets = columns * slot_total
+    inner_rows = inner_quad.shape[1]
     position = jnp.arange(strip_rows, dtype=jnp.int32)
-    bucket = jnp.where(
-        position < strip_count[0, 0], strip_dest[0, :, 0] * slot_total + strip_target[0], buckets
-    )
-    outgoing = bucket_sums(
-        strip_quad[0], strip_weight[0], bucket, buckets, slot_total, jnp.bfloat16
-    )
-    inner_sum = bucket_sums(
-        inner_quad[0], inner_weight[0], inner_target[0], slot_total, slot_total // 2, jnp.float32
-    )
+    strip_plan = grouped(
+        strip_dest[0, :, 0],
+        strip_target[0],
+        position < strip_count[0, 0],
+        columns,
+        3 * strip_rows // (2 * columns),
+        slot_total,
+    )
+    pieces = 4
+    piece = inner_rows // pieces
+    position = jnp.arange(inner_rows, dtype=jnp.int32)
+    inner_plan = grouped(
+        position // piece, inner_target[0], position >= 0, pieces, piece, slot_total
+    )
+    roots = tuple(jnp.sqrt(weight[0])[:, None, :] for weight in (strip_weight, inner_weight))
     pick = (jnp.arange(row_total, dtype=jnp.int32)[:, None] == coarse_owner[0][None, :]).astype(
         jnp.float32
     )
     assembled, coarse, panel_matrix = exchange(
-        outgoing, inner_sum, pick, panel_shift[0], columns, row_total
+        (strip_quad[0], inner_quad[0]), roots, strip_plan, inner_plan, pick, panel_shift[0],
+        columns, row_total,
     )
     factor = jnp.linalg.cholesky(panel_matrix)
     return (

time: 185 us -> 149 us (0.81)
  Pallas kernels: 161 us -> 113 us
  local copies, waits for them, and re-layouts: 4.71 us -> 11 us
  other arithmetic: 17.7 us -> 22.9 us
    pallas_call x2 -> x0, Pallas kernels: 54.3 us -> none  [bucket_sums(): pl.pallas_call(functools.partial(tangent_kernel, group), out_shape=jax.Sh...]
    pallas_call x1, Pallas kernels: 107 us -> 113 us  [exchange(): pl.pallas_call(functools.partial(exchange_kernel, outer, inner_size, rows...]
    sqrt x0 -> x2, local copies, waits for them, and re-layouts: none -> 1.89 us  [body(): jnp.sqrt(weight[0])[:, None, :]]
    unnamed x2 -> x4, local copies, waits for them, and re-layouts: 3.78 us -> 5.36 us
where the time goes in v2:
time: 149 us
  Pallas kernels  113 us (76%)
  other arithmetic  22.9 us (15%)
  local copies, waits for them, and re-layouts  11 us (7%)
    pallas_call x1, Pallas kernels, exchange(): pl.pallas_call(functools.partial(exchange_kernel, outer, inner_size, rows...  113 us
    another operation x3, other arithmetic, body(): factor = jnp.linalg.cholesky(panel_matrix)  12.4 us
    unnamed x4, local copies, waits for them, and re-layouts  5.36 us

profile of v2, /device:TPU:1, one launch (start us, length us, event | category | flops | bytes accessed | tf_op | source)
XLA Modules:
  0.0 148.7 jit_solution(4367025715550740048)
XLA Ops:
  1.3 0.7 bitcast_add_fusion.2
  2.0 0.7 fusion.10
  3.0 0.7 max.17.inner_last
  3.7 0.7 reshape.261.inner_some
  4.4 1.3 fusion.6.pick_ref
  6.4 0.7 pad_convert_fusion.1.inner_same
  7.0 0.7 compare_select_fusion
  8.0 1.0 convert_reduce_fusion.2
  8.9 0.7 add_select_fusion.4
  9.9 0.7 max.15.strip_last
  10.5 0.7 reshape.260.strip_some
  11.9 0.7 pad_convert_fusion.strip_same
  12.5 0.9 sqrt.31
  13.5 0.7 copy.20
  14.2 1.0 sqrt.30
  15.2 0.8 copy.19
  16.0 113.4 %shard_map.121 = (bf16[32,128,128]{2,1,0:T(8,128)(2,1)}, f32[128,128]{1,0:T(8,128)}, f32[128,128]{1,0:T(8,128)}) custom-call(bf16[256,192,128]{2,1,0:T(8,128)(2,1)} %bitcast.32, bf16[128,192,128]{2,1,0:T(8,128)(2,1)} %bitcast.33, f32[256,1,192]{2,1,0:T(1,128)} %bitcast.34, f32[128,1,192]{2,1,0:T(1,128)} %bitcast.36, s32[8,48]{1,0:T(8,128)} %get-tuple-element.14.strip_order, ...), custom_call_target="tpu_custom_call" | custom-call | tf_op jit(solution)/shard_map/pallas_call | solution.py:275
  129.4 0.9 copy.18
  130.4 0.9 fusion.1
  131.2 11.7 %cholesky.18 = f32[128,128]{1,0:T(8,128)S(1)} custom-call(f32[128,128]{1,0:T(8,128)S(1)} %fusion.1), custom_call_target="Cholesky" | custom-call | tf_op jit(solution)/shard_map/jit(cholesky)/cholesky | solution.py:356
  143.0 0.6 compare_reduce_fusion
  143.6 1.3 select_bitcast_fusion
  144.9 2.3 %copy.24 = bf16[1,32,128,128]{3,2,1,0:T(8,128)(2,1)} copy(bf16[1,32,128,128]{3,2,1,0:T(8,128)(2,1)} %bitcast.35) | data formatting | bytes 2097152
  147.2 1.5 copy.25
  (21 shorter events, 2.3 us)

commit v3 on v2

--- a/solution.py
+++ b/solution.py
@@ -9,41 +9,32 @@
 MESH = pl.DeviceIdType.MESH
 VMEM_LIMIT = 60 * 1024 * 1024
 UNROLL = 8
+SPAN = 1024
 
 
 def grouped(member, target, valid, groups, capacity, slots):
     count = member.shape[0]
     place = jnp.arange(count, dtype=jnp.int32)
-    key = target * count + place
+    key = target * SPAN + place
     peer = (member[:, None] == member[None, :]) & valid[None, :]
     rank = jnp.sum((peer & (key[None, :] < key[:, None])).astype(jnp.int32), axis=1)
     spot = jnp.where(valid, member * capacity + rank, groups * capacity)
     at = spot[None, :] == jnp.arange(groups * capacity, dtype=jnp.int32)[:, None]
     packed = jnp.sum(jnp.where(at, key[None, :], 0), axis=1).reshape(groups, capacity)
-    order, label = packed % count, packed // count
-    same = jnp.concatenate(
-        [jnp.zeros((groups, 1), jnp.bool_), label[:, 1:] == label[:, :-1]], axis=1
-    ).astype(jnp.float32)
-    bucket = jnp.where(valid, member * slots + target, groups * slots)
-    index = jnp.arange(groups * slots, dtype=jnp.int32)[:, None]
-    held = jnp.sum((bucket[None, :] == index).astype(jnp.int32), axis=1)
-    upto = jnp.sum(
-        ((bucket[None, :] <= index) & (bucket[None, :] >= index // slots * slots)).astype(
-            jnp.int32
-        ),
-        axis=1,
-    )
-    last = jnp.maximum(upto - 1, 0).reshape(groups, slots)
-    some = (held > 0).astype(jnp.float32).reshape(groups, slots)
-    return order, same, last, some
+    bucket = jnp.where(valid, member * slots + target, groups * slots)[None, None, :]
+    index = jnp.arange(groups * slots, dtype=jnp.int32).reshape(groups, slots, 1)
+    first = jnp.arange(groups, dtype=jnp.int32)[:, None, None] * slots
+    at_or_before = (bucket <= index) & (bucket >= first)
+    coded = at_or_before.astype(jnp.int32) + (bucket == index).astype(jnp.int32) * SPAN
+    coded = jnp.sum(coded, axis=2)
+    last = jnp.where(coded >= SPAN, coded % SPAN - 1, -1)
+    return packed, last
 
 
 def exchange_kernel(
-    outer, inner_size, rows,
+    outer, inner_size, rows, capacity, pieces,
     strip_ref, inner_ref, strip_root, inner_root,
-    strip_order, strip_same, strip_last, strip_some,
-    inner_order, inner_same, inner_last, inner_some,
-    pick_ref, shift_ref,
+    order_ref, last_ref, owner_ref, shift_ref,
     assembled_ref, coarse_ref, panel_ref,
     quad, run, out, tot, near, line_out, line_in, part, part_in,
     load_sem, near_send, near_recv, line_send, line_recv, part_send, part_recv,
@@ -85,20 +76,37 @@
 
     owners = [owner(s) for s in range(outer)]
 
-    def sum_runs(root, order, same, g):
-        def step(i, total):
+    def sum_runs(root, base, length, g):
+        def step(i, carry):
+            total, before = carry
             for j in range(UNROLL):
                 p = i * UNROLL + j
-                n = order[g, p]
-                scaled = (quad[n].T.astype(f32) * root[n]).astype(jnp.bfloat16)
+                key = order_ref[g, p]
+                n = jnp.maximum(key % SPAN - base, 0)
+                label = key // SPAN
+                scaled = (quad[n].T.astype(f32) * jnp.sqrt(root[n])).astype(jnp.bfloat16)
                 tangent = lax.dot_general(
                     scaled, scaled, (((1,), (1,)), ((), ())), preferred_element_type=f32
                 )
-                total = total * same[g, p] + tangent
+                total = total * (label == before).astype(f32) + tangent
                 run[p] = total
-            return total
-
-        lax.fori_loop(0, order.shape[1] // UNROLL, step, jnp.zeros((width, width), f32))
+                before = label
+            return total, before
+
+        start = (jnp.zeros((width, width), f32), jnp.int32(-1))
+        lax.fori_loop(0, length // UNROLL, step, start)
+
+    def slot_sum(g, k):
+        end = last_ref[g, k]
+        return run[jnp.maximum(end, 0)] * (end >= 0).astype(f32)
+
+    @pl.when(a == 0)
+    def _():
+        line_in[0, a] = jnp.zeros(line_in.shape[2:], line_in.dtype)
+
+    @pl.when(a == outer - 1)
+    def _():
+        line_in[1, a] = jnp.zeros(line_in.shape[2:], line_in.dtype)
 
     load.wait()
     near_copies = []
@@ -107,12 +115,11 @@
         for j in range(1, inner_size):
             peer = (b + j) % inner_size
             target = owners[s] * inner_size + peer
-            sum_runs(strip_root, strip_order, strip_same, target)
+            sum_runs(strip_root, 0, capacity, target)
 
             @pl.loop(0, slots)
             def _(k):
-                value = run[strip_last[target, k]] * strip_some[target, k]
-                out[j - 1, s, k] = value.astype(out.dtype)
+                out[j - 1, s, k] = slot_sum(target, k).astype(out.dtype)
 
             copy = pltpu.make_async_remote_copy(
                 src_ref=out.at[j - 1, s],
@@ -127,8 +134,7 @@
         near_copies.append(group)
 
     def local(s, k):
-        mine = owners[s] * inner_size + b
-        value = run[strip_last[mine, k]] * strip_some[mine, k]
+        value = slot_sum(owners[s] * inner_size + b, k)
         for j in range(inner_size - 1):
             value = value + near[j, s, k].astype(f32)
         return value
@@ -148,7 +154,7 @@
             device_id=(row, after * inner_size + b),
             device_id_type=MESH,
         )
-        sum_runs(strip_root, strip_order, strip_same, target * inner_size + b)
+        sum_runs(strip_root, 0, capacity, target * inner_size + b)
         for near_copy in near_copies[s]:
             near_copy.wait_recv()
 
@@ -171,31 +177,27 @@
         line_copies.append(copy)
 
     last = outer - 1
-    sum_runs(strip_root, strip_order, strip_same, col)
+    sum_runs(strip_root, 0, capacity, col)
 
     @pl.loop(0, slots)
     def _(k):
-        tot[k] = run[strip_last[col, k]] * strip_some[col, k]
+        tot[k] = slot_sum(col, k)
 
     load = pltpu.make_async_copy(inner_ref, quad.at[pl.ds(0, inner_ref.shape[0])], load_sem.at[1])
     load.start()
     load.wait()
 
-    @pl.loop(0, inner_order.shape[0])
+    columns = outer * inner_size
+
+    @pl.loop(columns, columns + pieces)
     def _(g):
-        sum_runs(inner_root, inner_order, inner_same, g)
+        sum_runs(inner_root, strip_ref.shape[0], inner_ref.shape[0] // pieces, g)
 
         @pl.loop(0, slots)
         def _(k):
-            tot[k] += run[inner_last[g, k]] * inner_some[g, k]
-
-    for near_copy in near_copies[last]:
-        near_copy.wait_recv()
-
-    @pl.loop(0, slots)
-    def _(k):
-        for j in range(inner_size - 1):
-            tot[k] += near[j, last, k].astype(f32)
+            tot[k] += slot_sum(g, k)
+
+    part[...] = jnp.zeros_like(part)
 
     for way, there in ((0, a > 0), (1, a < outer - 1)):
 
@@ -210,19 +212,19 @@
                 device_id_type=MESH,
             ).wait_recv()
 
-            @pl.loop(0, slots)
-            def _(k):
-                tot[k] = tot[k] + line_in[way, a, k].astype(f32)
-
-    part[...] = jnp.zeros_like(part)
+    for near_copy in near_copies[last]:
+        near_copy.wait_recv()
 
     @pl.loop(0, slots)
     def _(k):
-        block = tot[k].astype(jnp.bfloat16)
+        value = tot[k] + line_in[0, a, k].astype(f32) + line_in[1, a, k].astype(f32)
+        for j in range(inner_size - 1):
+            value = value + near[j, last, k].astype(f32)
+        block = value.astype(jnp.bfloat16)
         assembled_ref[k] = block
         value = block.astype(f32)
         for r in range(rows):
-            part[r] += pick_ref[r, k] * value
+            part[r] += (owner_ref[0, k] == r).astype(f32) * value
 
     part_copies = []
     for j in range(1, rows):
@@ -259,10 +261,10 @@
         copy.wait_send()
 
 
-def exchange(quads, roots, strip_plan, inner_plan, pick, shift, columns, rows):
-    slots = pick.shape[1]
+def exchange(quads, weights, plan, owner, shift, capacity, pieces, columns, rows):
+    slots = owner.shape[1]
     width = shift.shape[1]
-    longest = max(strip_plan[0].shape[1], inner_plan[0].shape[1])
+    longest = plan[0].shape[1]
     outer = 4
     inner_size = columns // outer
     f32, bf16 = jnp.float32, jnp.bfloat16
@@ -273,7 +275,7 @@
     peers = max(1, rows - 1)
     vmem = pl.BlockSpec(memory_space=pltpu.VMEM)
     return pl.pallas_call(
-        functools.partial(exchange_kernel, outer, inner_size, rows),
+        functools.partial(exchange_kernel, outer, inner_size, rows, capacity, pieces),
         out_shape=(
             jax.ShapeDtypeStruct(block, bf16),
             jax.ShapeDtypeStruct((width, width), f32),
@@ -285,7 +287,7 @@
             vmem,
             vmem,
         ]
-        + [pl.BlockSpec(memory_space=pltpu.SMEM)] * 9
+        + [pl.BlockSpec(memory_space=pltpu.SMEM)] * 3
         + [vmem],
         out_specs=(vmem, vmem, vmem),
         scratch_shapes=[
@@ -309,7 +311,7 @@
         compiler_params=pltpu.CompilerParams(
             collective_id=0, has_side_effects=True, vmem_limit_bytes=VMEM_LIMIT
         ),
-    )(*quads, *roots, *strip_plan, *inner_plan, pick, shift)
+    )(*quads, *weights, *plan, owner, shift)
 
 
 def body(
@@ -330,30 +332,25 @@
     columns = lax.axis_size("pcol")
     row_total = lax.axis_size("prow")
     inner_rows = inner_quad.shape[1]
-    position = jnp.arange(strip_rows, dtype=jnp.int32)
-    strip_plan = grouped(
-        strip_dest[0, :, 0],
-        strip_target[0],
-        position < strip_count[0, 0],
-        columns,
-        3 * strip_rows // (2 * columns),
-        slot_total,
-    )
     pieces = 4
     piece = inner_rows // pieces
-    position = jnp.arange(inner_rows, dtype=jnp.int32)
-    inner_plan = grouped(
-        position // piece, inner_target[0], position >= 0, pieces, piece, slot_total
-    )
-    roots = tuple(jnp.sqrt(weight[0])[:, None, :] for weight in (strip_weight, inner_weight))
-    pick = (jnp.arange(row_total, dtype=jnp.int32)[:, None] == coarse_owner[0][None, :]).astype(
-        jnp.float32
-    )
+    capacity = 3 * strip_rows // (2 * columns)
+    position = jnp.arange(strip_rows, dtype=jnp.int32)
+    place = jnp.arange(inner_rows, dtype=jnp.int32)
+    plan = grouped(
+        jnp.concatenate([strip_dest[0, :, 0], columns + place // piece]),
+        jnp.concatenate([strip_target[0], inner_target[0]]),
+        jnp.concatenate([position < strip_count[0, 0], place >= 0]),
+        columns + pieces,
+        max(capacity, piece),
+        slot_total,
+    )
+    weights = tuple(weight[0][:, None, :] for weight in (strip_weight, inner_weight))
     assembled, coarse, panel_matrix = exchange(
-        (strip_quad[0], inner_quad[0]), roots, strip_plan, inner_plan, pick, panel_shift[0],
-        columns, row_total,
-    )
-    factor = jnp.linalg.cholesky(panel_matrix)
+        (strip_quad[0], inner_quad[0]), weights, plan, coarse_owner, panel_shift[0],
+        capacity, pieces, columns, row_total,
+    )
+    factor = lax.linalg.cholesky(panel_matrix, symmetrize_input=False)
     return (
         assembled.reshape(1, slot_total, width, width),
         coarse.reshape(1, 1, width, width),

time: 149 us -> 141 us (0.946)
  other arithmetic: 22.9 us -> 17.6 us
  local copies, waits for them, and re-layouts: 11 us -> 7.86 us
    convert_element_type x5 -> x0, other arithmetic: 2.6 us -> none  [the longest x2 1.34 us: grouped(): same = jnp.concatenate([jnp.zeros((groups, 1), jnp.bool_), label[:, 1:] =...]
    sqrt x2 -> x0, local copies, waits for them, and re-layouts: 1.89 us -> none  [body(): jnp.sqrt(weight[0])[:, None, :]]
    unnamed x4, local copies, waits for them, and re-layouts: 5.36 us -> 7.18 us
where the time goes in v3:
time: 141 us; the launch traced here: 140 us
  Pallas kernels  114 us (81%)
  other arithmetic  17.6 us (12%)
  local copies, waits for them, and re-layouts  7.86 us (6%)
    pallas_call x1, Pallas kernels, exchange(): pl.pallas_call(functools.partial(exchange_kernel, outer, inner_size, rows...  114 us
    another operation x3, other arithmetic, body(): factor = lax.linalg.cholesky(panel_matrix, symmetrize_input=False)  13.2 us
    unnamed x4, local copies, waits for them, and re-layouts  7.18 us

profile of v3, /device:TPU:1, one launch (start us, length us, event | category | flops | bytes accessed | tf_op | source)
XLA Modules:
  0.0 140.3 jit_solution(4870335636198793387)
XLA Ops:
  1.3 0.7 pad_add_fusion
  2.0 0.3 convert_reduce_fusion
  2.3 0.7 add_select_fusion.1
  3.1 0.2 select_reduce_fusion
  3.3 0.7 reshape.120.order_ref
  3.9 0.1 broadcast_compare_fusion
  4.0 0.4 add_reduce_fusion
  4.4 0.6 fusion.2.last_ref
  5.0 1.6 %copy.16 = f32[1,128,192]{2,0,1:T(1,128)} copy(f32[1,128,192]{1,2,0:T(8,128)} %param.16) | data formatting | bytes 196608 | tf_op args[6]
  6.7 1.8 %copy.15 = f32[1,256,192]{2,0,1:T(1,128)} copy(f32[1,256,192]{1,2,0:T(8,128)} %param.11) | data formatting | bytes 393216 | tf_op args[1]
  8.4 113.6 %shard_map.121 = (bf16[32,128,128]{2,1,0:T(8,128)(2,1)}, f32[128,128]{1,0:T(8,128)}, f32[128,128]{1,0:T(8,128)}) custom-call(bf16[256,192,128]{2,1,0:T(8,128)(2,1)} %bitcast.14, bf16[128,192,128]{2,1,0:T(8,128)(2,1)} %bitcast.15, f32[256,1,192]{2,1,0:T(1,128)} %bitcast.16, f32[128,1,192]{2,1,0:T(1,128)} %bitcast.18, s32[12,48]{1,0:T(8,128)} %reshape.120.order_ref, ...), custom_call_target="tpu_custom_call" | custom-call | tf_op jit(solution)/shard_map/pallas_call | solution.py:277
  122.0 12.5 %cholesky.18 = f32[128,128]{1,0:T(8,128)S(1)} custom-call(f32[128,128]{1,0:T(8,128)} %get-tuple-element.8), custom_call_target="Cholesky" | custom-call | tf_op jit(solution)/shard_map/cholesky | solution.py:353
  134.6 0.6 compare_reduce_fusion
  135.2 1.3 select_bitcast_fusion
  136.5 2.3 %copy.20 = bf16[1,32,128,128]{3,2,1,0:T(8,128)(2,1)} copy(bf16[1,32,128,128]{3,2,1,0:T(8,128)(2,1)} %bitcast.17) | data formatting | bytes 2097152
  138.8 1.5 %copy.21 = f32[1,1,128,128]{3,2,1,0:T(8,128)} copy(f32[1,1,128,128]{3,2,1,0:T(8,128)} %bitcast.19) | data formatting | bytes 131072
  (6 shorter events, 0.1 us)
